TPU v7x, 128 devices: a whole 4x4x4 slice. The times are simulated.
128 devices in a mesh: beam: 64 (over z_lo, y, x, core), row: 2 (over z_hi).
Axes of the slice: x: 4, y: 4, z: 4 (z_hi: 2, z_lo: 2; z = z_hi * 2 + z_lo), core: 2. Of those that a mesh axis runs over, the one named last changes fastest.
Arguments:
- tilts: int32 [128, 2], P('beam'), may hold values from -64 to 64
- potentials: bfloat16 [64, 1024, 1024], P('beam', 'row'), may hold values from 0 to 2
- owners: int32 [2], replicated, may hold values from 0 to 63
- beam_amplitude: float32 [128], P('beam'), may hold values from 0.5 to 1.5
- beam_phase: float32 [128], P('beam'), may hold values from -3.140625 to 3.140625
- probe_positions: int32 [128, 2], replicated, may hold values from 0 to 1023, as said below
- beam_offsets: int32 [128], replicated, may hold values from 0 to 127
Outputs:
- exit_waves: bfloat16 [128, 1024, 2048], P('beam', 'row')
- probe_waves: float32 [2, 64, 64, 128], P('row', 'beam')
Inputs may be any that keep to these rules, and one draw needn't show every extreme that they name: `probe_positions`: probe p's row coordinate Y_p lies in rows (p // 64) * 512 to (p // 64 + 1) * 512 - 1; its column coordinate is any pixel.
All inputs are finite; a program needn't handle non-finite values.
Results may differ from a plain program's by a relative error of at most 0.0073.
Values may be sent and summed in bfloat16 or wider, within the bound.
A program may use at most 128 MiB of HBM per device.

v0:
```python
import math

import jax
import jax.numpy as jnp
import numpy as np
from jax import lax
from jax.sharding import PartitionSpec as P

SLICES = 2
RAD = 8
WIN = 64


ROW_CHIRP = 0.07


def spread_2(value, axis, source):
    kept = jnp.where(lax.axis_index(axis) == source, value, 0).astype(value.dtype)
    return lax.psum(kept, axis)


def extended_2(block, sides, width):
    for axis, dim in sides:
        count = lax.axis_size(axis)
        forward = [(i, i + 1) for i in range(count - 1)]
        forward.append((count - 1, 0))
        backward = [(target, source) for source, target in forward]
        low = lax.ppermute(
            lax.slice_in_dim(block, block.shape[dim] - width, None, axis=dim), axis, forward
        )
        high = lax.ppermute(lax.slice_in_dim(block, 0, width, axis=dim), axis, backward)
        block = jnp.concatenate([low, block, high], axis=dim)
    return block


def fresnel_matrix(pixel_count):
    frequency = np.arange(pixel_count) - pixel_count // 2
    passband = (np.abs(frequency) * 3 <= pixel_count) * 1.0
    phases = -6.0 * math.pi * (3.0 * frequency / pixel_count) ** 2
    spec_real = passband * np.cos(phases)
    spec_imag = passband * np.sin(phases)
    steps_n = np.arange(pixel_count)
    turns = np.mod(frequency[:, None] * steps_n[None, :], pixel_count) * (
        2.0 * math.pi / pixel_count
    )
    cos_table = np.cos(turns)
    sin_table = np.sin(turns)
    kernel_real = (spec_real @ cos_table - spec_imag @ sin_table) / pixel_count
    kernel_imag = (spec_real @ sin_table + spec_imag @ cos_table) / pixel_count
    distance = (np.arange(pixel_count)[None, :] - np.arange(pixel_count)[:, None]) % pixel_count
    circ_real = kernel_real[distance]
    circ_imag = kernel_imag[distance]
    upper_half = np.concatenate([circ_real, circ_imag], axis=1)
    lower_half = np.concatenate([-circ_imag, circ_real], axis=1)
    return np.concatenate([upper_half, lower_half], axis=0).astype(jnp.float32)


def row_taps(radius):
    distance = np.arange(-radius, radius + 1) * 1.0
    envelope = np.exp(-0.5 * (distance / radius) ** 2)
    angle_table = math.pi * ROW_CHIRP * distance**2
    norm_value = np.sqrt(np.sum(envelope**2))
    taps_real = envelope * np.cos(angle_table) / norm_value
    taps_imag = envelope * np.sin(angle_table) / norm_value
    return ([float(entry) for entry in taps_real], [float(entry) for entry in taps_imag])


def plane_waves(tilt_table, row_start, row_count, pixel_count):
    row_ids = row_start + jnp.arange(row_count, dtype=jnp.int32)
    column_ids = jnp.arange(pixel_count, dtype=jnp.int32)
    turns = jnp.mod(
        tilt_table[:, 0][:, None, None] * row_ids[None, :, None]
        + tilt_table[:, 1][:, None, None] * column_ids[None, None, :],
        pixel_count,
    )
    angles = turns.astype(jnp.float32) * (2.0 * math.pi / pixel_count)
    return jnp.concatenate([jnp.cos(angles), jnp.sin(angles)], axis=2)


def transmission(potential_tile):
    phases = potential_tile.astype(jnp.float32)
    return jnp.concatenate([jnp.cos(phases), jnp.sin(phases)], axis=-1).astype(jnp.bfloat16)


def transmit(wavefield, factor):
    pixel_count = wavefield.shape[-1] // 2
    wave_real = wavefield[..., :pixel_count]
    wave_imag = wavefield[..., pixel_count:]
    factor_real = factor[None, :, :pixel_count]
    factor_imag = factor[None, :, pixel_count:]
    product = jnp.concatenate(
        [
            wave_real * factor_real - wave_imag * factor_imag,
            wave_real * factor_imag + wave_imag * factor_real,
        ],
        axis=-1,
    )
    return product.astype(jnp.bfloat16)


def mix_padded(padded, taps_real, taps_imag, row_count):
    pixel_count = padded.shape[-1] // 2
    radius = (len(taps_real) - 1) // 2
    total_real = jnp.zeros((padded.shape[0], row_count, pixel_count), jnp.float32)
    total_imag = jnp.zeros((padded.shape[0], row_count, pixel_count), jnp.float32)
    for position in range(len(taps_real)):
        offset_rows = position - radius
        moved = padded[:, radius - offset_rows : radius - offset_rows + row_count]
        moved_real = moved[:, :, :pixel_count]
        moved_imag = moved[:, :, pixel_count:]
        total_real = (
            total_real + taps_real[position] * moved_real - taps_imag[position] * moved_imag
        )
        total_imag = (
            total_imag + taps_real[position] * moved_imag + taps_imag[position] * moved_real
        )
    return jnp.concatenate([total_real, total_imag], axis=2)


def coefficients(
    tilt_table, beam_ids, amplitude, phase, position, offset_value, beam_count, span, pixel_count
):
    turns = jnp.mod(tilt_table[:, 0] * position[0] + tilt_table[:, 1] * position[1], pixel_count)
    angles = phase - turns.astype(jnp.float32) * (2.0 * math.pi / pixel_count)
    inside = (jnp.mod(beam_ids - offset_value, beam_count) < span).astype(jnp.float32)
    weight = amplitude * inside * (1.0 / math.sqrt(span))
    return (weight * jnp.cos(angles), weight * jnp.sin(angles))


def combine(coeff_real, coeff_imag, real_window, imag_window):
    probe_real = jnp.einsum("b,bjk->jk", coeff_real, real_window) - jnp.einsum(
        "b,bjk->jk", coeff_imag, imag_window
    )
    probe_imag = jnp.einsum("b,bjk->jk", coeff_real, imag_window) + jnp.einsum(
        "b,bjk->jk", coeff_imag, real_window
    )
    return jnp.concatenate([probe_real, probe_imag], axis=1)


def widen_columns(extended, pixel_count):
    return jnp.concatenate(
        [
            extended[:, :, :pixel_count],
            extended[:, :, :WIN],
            extended[:, :, pixel_count:],
            extended[:, :, pixel_count : pixel_count + WIN],
        ],
        axis=2,
    )


def body(tilts, potentials, owners, beam_amplitude, beam_phase, probe_positions, beam_offsets):
    local_beams = tilts.shape[0]
    row_count = potentials.shape[1]
    pixel_count = potentials.shape[2]
    beam_devices = lax.axis_size("beam")
    row_devices = lax.axis_size("row")
    beam_count = local_beams * beam_devices
    span = beam_count // 2
    row_index = lax.axis_index("row")
    row_start = row_index * row_count
    beam_ids = lax.axis_index("beam") * local_beams + jnp.arange(local_beams, dtype=jnp.int32)
    matrix = jnp.asarray(fresnel_matrix(pixel_count)).astype(jnp.bfloat16)
    taps_real, taps_imag = row_taps(RAD)
    wavefield = plane_waves(tilts, row_start, row_count, pixel_count)
    for layer_index in range(SLICES):
        owner_index = owners[layer_index]
        factor = spread_2(transmission(potentials[0]), "beam", owner_index)
        transmitted = transmit(wavefield, factor)
        spread = jnp.einsum("brk,kl->brl", transmitted, matrix, preferred_element_type=jnp.float32)
        padded = extended_2(spread, (("row", 1),), RAD)
        wavefield = mix_padded(padded, taps_real, taps_imag, row_count)
    exit_waves = wavefield.astype(jnp.bfloat16)
    blank_rows = jnp.zeros((local_beams, WIN, 2 * pixel_count), jnp.bfloat16)
    widened = widen_columns(
        jnp.concatenate([blank_rows, exit_waves, blank_rows], axis=1), pixel_count
    )
    lead_rows = WIN
    probe_block = probe_positions.shape[0] // row_devices
    probe_share = probe_block // beam_devices

    def one_probe(position, offset_value):
        local_row = jnp.mod(position[0] - row_start + WIN, pixel_count) - WIN
        valid = ((local_row >= 0 - lead_rows) & (local_row < row_count)).astype(jnp.float32)
        first_row = jnp.clip(local_row + lead_rows, 0, row_count + lead_rows - 1)
        real_window = lax.dynamic_slice(
            widened, (0, first_row, position[1]), (local_beams, WIN, WIN)
        ).astype(jnp.float32)
        imag_window = lax.dynamic_slice(
            widened, (0, first_row, pixel_count + WIN + position[1]), (local_beams, WIN, WIN)
        ).astype(jnp.float32)
        coeff_real, coeff_imag = coefficients(
            tilts,
            beam_ids,
            beam_amplitude,
            beam_phase,
            position,
            offset_value,
            beam_count,
            span,
            pixel_count,
        )
        return valid * combine(coeff_real, coeff_imag, real_window, imag_window)

    all_terms = jax.vmap(one_probe)(probe_positions, beam_offsets).reshape(
        row_devices, probe_block, WIN, 2 * WIN
    )
    folded = lax.psum_scatter(all_terms, "row", scatter_dimension=0, tiled=True)[0]
    summed = lax.psum_scatter(
        lax.slice_in_dim(folded, 0, lax.axis_size("beam") * probe_share, axis=0),
        "beam",
        scatter_dimension=0,
        tiled=True,
    )
    return (exit_waves, summed[None])


def solution(mesh):
    return jax.shard_map(
        body,
        mesh=mesh,
        in_specs=(P("beam", None), P("beam", "row", None), P(), P("beam"), P("beam"), P(), P()),
        out_specs=(P("beam", "row", None), P("row", "beam", None, None)),
        check_vma=False,
    )
```

profile of v0, /device:TPU:1, one launch (start us, length us, event | category | flops | bytes accessed | tf_op | source)
XLA Modules:
  0.0 2102.7 jit_solution(2879608918873955339)
XLA Ops:
  9.8 8.4 fusion.76
  18.3 3.0 broadcast_select_fusion
  22.2 561.6 %all-reduce.3.cloned.1.call-done = (bf16[512,2048]{1,0:T(8,128)(2,1)}, bf16[512,2048]{1,0:T(8,128)(2,1)}) async-done(((bf16[512,2048]{1,0:T(8,128)(2,1)}, bf16[512,2048]{1,0:T(8,128)(2,1)}), (bf16[512,2048]{1,0:T(8,128)(2,1)}, bf16[512,2048]{1,0:T(8,128)(2,1)})) %all-reduce.3.cloned.1.call-update) | async-done | bytes 4194320 | tf_op jit(solution)/shard_map/psum | solution.py:19
  585.8 18.1 subtract_convert_fusion.2
  604.0 11.4 fusion.63
  615.4 2.7 collective-permute-start
  621.2 2.4 collective-permute-done.1
  623.6 39.7 %subtract_convert_fusion.1 = (bf16[2,512,1024]{2,1,0:T(8,128)(2,1)S(1)}, f32[2,512,1024]{2,1,0:T(8,128)S(1)}, f32[2,512,1024]{2,1,0:T(8,128)}) fusion(f32[512,1024]{1,0:T(8,128)S(1)} %get-tuple-element.58, f32[512,1024]{1,0:T(8,128)S(1)} %get-tuple-element.57, f32[2,512,2048]{2,1,0:T(8,128)S(1)} %fusion.63, f32[2,8,2048]{2,1,0:T(8,128)S(1)} %collective-permute-done.1, ...), kind=kLoop, calls=%fused_computation.152 | loop fusion | flops 209715200 | bytes 31719424 | tf_op jit(solution)/shard_map/convert.2
  663.3 3.8 add_convert_fusion.1
  667.1 11.2 fusion.67
  678.4 3.3 copy-done
  681.7 2.6 collective-permute-start.2
  687.1 4.2 collective-permute-done.3
  691.3 56.4 %subtract_convert_fusion = bf16[2,512,1024]{2,1,0:T(8,128)(2,1)S(1)} fusion(f32[2,512,2048]{2,1,0:T(8,128)} %copy-done, f32[2,8,2048]{2,1,0:T(8,128)S(1)} %collective-permute-done.2, f32[2,8,2048]{2,1,0:T(8,128)S(1)} %collective-permute-done.3), kind=kLoop, calls=%fused_computation.150 | loop fusion | flops 104857600 | bytes 19136512 | tf_op jit(solution)/shard_map/convert
  747.7 19.2 add_convert_fusion
  767.2 5.6 pad_maximum_fusion
  772.8 3.0 fusion.95
  775.8 10.2 concatenate.88
  786.0 6.2 broadcast.237.clone2.1
  792.2 466.4 %while.2 = (s32[]{:T(128)}, bf16[2,640,2176]{2,1,0:T(8,128)(2,1)}, s32[128,3]{0,1:T(4,128)S(1)}, bf16[128,2,64,64]{3,1,2,0:T(2,128)(2,1)}, s32[]{:T(128)}) while((s32[]{:T(128)}, bf16[2,640,2176]{2,1,0:T(8,128)(2,1)}, s32[128,3]{0,1:T(4,128)S(1)}, bf16[128,2,64,64]{3,1,2,0:T(2,128)(2,1)}, s32[]{:T(128)}) %tuple.60), condition=%wide.while_cond, body=%wide.while_body.sunk | while | flops 2 | bytes 82545 | solution.py:186
  803.8 2.3 dynamic-slice_bitcast_fusion.4
  807.4 2.3 dynamic-slice_bitcast_fusion.4
  1258.6 6.2 broadcast.237.clone2
  1264.8 459.1 %while.3 = (s32[]{:T(128)}, bf16[2,640,2176]{2,1,0:T(8,128)(2,1)}, s32[128,3]{0,1:T(4,128)S(1)}, bf16[128,2,64,64]{3,1,2,0:T(2,128)(2,1)}, s32[]{:T(128)}) while((s32[]{:T(128)}, bf16[2,640,2176]{2,1,0:T(8,128)(2,1)}, s32[128,3]{0,1:T(4,128)S(1)}, bf16[128,2,64,64]{3,1,2,0:T(2,128)(2,1)}, s32[]{:T(128)}) %tuple.70), condition=%wide.while_cond.1, body=%wide.while_body.1.sunk | while | flops 2 | bytes 82545 | solution.py:189
  1723.9 6.6 fusion.97
  1730.5 4.7 fusion.100
  1735.2 4.7 fusion.98
  1739.9 5.0 fusion.99
  1747.6 3.4 maximum_multiply_fusion
  1751.0 60.8 %reduce-scatter.3.cloned.1.call-done = f32[1,64,64,128]{3,2,1,0:T(8,128)} async-done(((f32[2,64,64,128]{3,2,1,0:T(8,128)}), f32[1,64,64,128]{3,2,1,0:T(8,128)}) %reduce-scatter.3.cloned.1.call-update) | async-done | bytes 2097168 | tf_op jit(solution)/shard_map/reduce_scatter | solution.py:208
  1811.8 4.1 pad_maximum_fusion.5
  1816.0 279.7 %reduce-scatter.5.cloned.1.call-done = f32[1,64,128]{2,1,0:T(8,128)} async-done(((f32[64,64,128]{2,1,0:T(8,128)}), f32[1,64,128]{2,1,0:T(8,128)}) %reduce-scatter.5.cloned.1.call-update) | async-done | bytes 32784 | tf_op jit(solution)/shard_map/reduce_scatter | solution.py:209
  (1073 shorter events, 933.4 us)
Async XLA Ops:
  7.2 576.7 %all-reduce.3.cloned.1.call-start = ((), (), s32[]{:S(2)}) async-start(), calls=%async_computation.4 | async-start | bytes 8388608 | tf_op jit(solution)/shard_map/psum | solution.py:19
  18.2 3.1 copy-start.7
  18.2 3.2 copy-start.6
  18.2 3.6 copy-start.8
  18.3 3.5 copy-start.9
  18.3 3.5 copy-start.10
  21.3 1790.5 %reduce-scatter.3.cloned.1.call-start = ((), (), s32[]{:S(2)}) async-start(), calls=%async_computation.2 | async-start | bytes 6291456 | tf_op jit(solution)/shard_map/reduce_scatter | solution.py:208
  603.9 14.7 copy-start.5
  615.4 5.8 collective-permute-start
  618.1 5.6 collective-permute-start.1
  678.4 3.3 copy-start
  681.7 5.4 collective-permute-start.2
  684.3 7.0 collective-permute-start.3
  691.3 56.4 %copy-start.1 = (f32[2,512,2048]{2,1,0:T(8,128)S(1)}, f32[2,512,2048]{2,1,0:T(8,128)}, u32[]{:S(2)}) copy-start(f32[2,512,2048]{2,1,0:T(8,128)} %copy-done) | copy-start | bytes 25165828
  767.0 5.9 copy-start.2
  1723.9 6.6 copy-start.4
  1730.5 4.7 copy-start.3
  1751.0 344.7 %reduce-scatter.5.cloned.1.call-start = ((), (), s32[]{:S(2)}) async-start(), calls=%async_computation.3 | async-start | bytes 2129920 | tf_op jit(solution)/shard_map/reduce_scatter | solution.py:209
Sparse Core Ops, SparseCore 0:
  21.4 562.3 all-reduce.2
  1751.1 60.6 reduce-scatter.2
  1814.7 280.8 reduce-scatter.4
where the time goes:
time: 2130 us; the launch traced here: 2100 us
  local copies, waits for them, and re-layouts  955 us (45%)
  waiting for transfers between devices  913 us (43%)
  other arithmetic  168 us (8%)
  matrix products  43.5 us (2%)
    gather x1024, local copies, waits for them, and re-layouts  925 us
    psum x1, waiting for transfers between devices, spread_2(): return lax.psum(kept, axis)  562 us
    reduce_scatter x1, waiting for transfers between devices, body(): lax.psum_scatter(lax.slice_in_dim(folded, 0, lax.axis_size('beam') * prob...  280 us
    another operation x5, other arithmetic  137 us
    reduce_scatter x1, waiting for transfers between devices, body(): lax.psum_scatter(all_terms, 'row', scatter_dimension=0, tiled=True)[0]  60.8 us
  transfers between devices with their start and end apart: 7, of which 7 were waited for; matrix products, arithmetic and copies ran while one was open for 0% of the time, Pallas kernels for 0%

commit v1 on v0

v1 whole, which is shorter than its diff:
```python
import math

import jax
import jax.numpy as jnp
import ml_dtypes
import numpy as np
from jax import lax
from jax.experimental import pallas as pl
from jax.experimental.pallas import tpu as pltpu
from jax.sharding import PartitionSpec as P

NPIX = 1024
RAD = 8
WIN = 64
ROW_CHIRP = 0.07
QUARTER = NPIX // 4
LANES = 128
STRIPS = NPIX // LANES
BEFORE = 2 * RAD
AFTER = 80
KEPT = BEFORE + NPIX // 2 + AFTER
BLOCK_IN = 128
BLOCK = BLOCK_IN - 2 * RAD
FULL_BLOCKS = 4
TAIL = FULL_BLOCKS * BLOCK
PASSED = TAIL + BLOCK_IN - 6 * RAD
STEP = 48
F32 = jnp.float32
BF16 = jnp.bfloat16
MESH = pl.DeviceIdType.MESH


def row_taps():
    distance = np.arange(-RAD, RAD + 1) * 1.0
    envelope = np.exp(-0.5 * (distance / RAD) ** 2)
    angles = math.pi * ROW_CHIRP * distance**2
    norm = np.sqrt(np.sum(envelope**2))
    return envelope * np.cos(angles) / norm, envelope * np.sin(angles) / norm


def row_matrices():
    taps_real, taps_imag = row_taps()
    real = np.zeros((BLOCK, BLOCK_IN))
    imag = np.zeros((BLOCK, BLOCK_IN))
    for out in range(BLOCK):
        for position in range(2 * RAD + 1):
            offset = position - RAD
            real[out, out + RAD - offset] = taps_real[position]
            imag[out, out + RAD - offset] = taps_imag[position]
    return real.astype(np.float32), imag.astype(np.float32)


def ring_matrices():
    frequency = np.arange(NPIX) - NPIX // 2
    passband = (np.abs(frequency) * 3 <= NPIX) * 1.0
    phases = -6.0 * math.pi * (3.0 * frequency / NPIX) ** 2
    turns = np.mod(frequency[:, None] * np.arange(NPIX)[None, :], NPIX) * (2.0 * math.pi / NPIX)
    spectrum = passband * np.exp(1j * phases)
    kernel = (spectrum @ np.exp(1j * turns)) / NPIX
    held_real = kernel.real.astype(np.float32).astype(ml_dtypes.bfloat16).astype(np.float64)
    held_imag = kernel.imag.astype(np.float32).astype(ml_dtypes.bfloat16).astype(np.float64)
    quarters = (held_real + 1j * held_imag).reshape(4, QUARTER)
    steps = np.arange(QUARTER)[None, :] - np.arange(QUARTER)[:, None]
    matrices = []
    for ring in range(4):
        root = 1j**ring
        folded = sum(root**part * quarters[part] for part in range(4)) / 4.0
        matrix = np.where(steps >= 0, 1.0, root) * folded[steps % QUARTER]
        matrices.append(
            np.block([[matrix.real, matrix.imag], [-matrix.imag, matrix.real]]).astype(np.float32)
        )
    return np.stack(matrices).astype(ml_dtypes.bfloat16)


def fitted(function, degree, reach=1.0):
    nodes = reach * np.cos(np.pi * (np.arange(64) + 0.5) / 64)
    powers = np.stack([nodes**power for power in degree], axis=1)
    return [float(c) for c in np.linalg.lstsq(powers, function(nodes), rcond=None)[0]]


def polynomial(coefficients, square):
    total = coefficients[-1]
    for c in coefficients[-2::-1]:
        total = total * square + c
    return total


EVEN = fitted(np.cos, (0, 2, 4, 6, 8))
ODD = fitted(np.sin, (1, 3, 5, 7))
TURN_EVEN = fitted(lambda u: np.cos(2 * np.pi * u), range(0, 17, 2), 0.5)
TURN_ODD = fitted(lambda u: np.sin(2 * np.pi * u), range(1, 18, 2), 0.5)


def circle(turns):
    square = turns * turns
    return polynomial(TURN_EVEN, square), polynomial(TURN_ODD, square) * turns


def phasor(steps):
    return circle((((steps + NPIX // 2) & (NPIX - 1)) - NPIX // 2).astype(F32) * (1.0 / NPIX))


def cos_sin(values):
    shifted = values - 1.0
    square = shifted * shifted
    even = polynomial(EVEN, square)
    odd = polynomial(ODD, square) * shifted
    c1, s1 = math.cos(1.0), math.sin(1.0)
    return c1 * even - s1 * odd, s1 * even + c1 * odd


def dot(a, b):
    return jnp.dot(a, b, preferred_element_type=F32)


def split(real, imag):
    r = [real[:, q * QUARTER : (q + 1) * QUARTER] for q in range(4)]
    i = [imag[:, q * QUARTER : (q + 1) * QUARTER] for q in range(4)]
    ar, ai, br, bi = r[0] + r[2], i[0] + i[2], r[0] - r[2], i[0] - i[2]
    cr, ci, dr, di = r[1] + r[3], i[1] + i[3], r[1] - r[3], i[1] - i[3]
    pairs = ((ar + cr, ai + ci), (br - di, bi + dr), (ar - cr, ai - ci), (br + di, bi - dr))
    return [jnp.concatenate([p.astype(BF16), q.astype(BF16)], axis=1) for p, q in pairs]


def join(products):
    r = [p[:, :QUARTER] for p in products]
    i = [p[:, QUARTER:] for p in products]
    ar, ai, br, bi = r[0] + r[2], i[0] + i[2], r[0] - r[2], i[0] - i[2]
    cr, ci, dr, di = r[1] + r[3], i[1] + i[3], r[1] - r[3], i[1] - i[3]
    return ((ar + cr, ai + ci), (br + di, bi - dr), (ar - cr, ai - ci), (br - di, bi + dr))


def propagate(parts, rings):
    return join([dot(jnp.concatenate(p, axis=0), rings[j]) for j, p in enumerate(zip(*parts))])


def first_kernel(
    owners,
    tilts,
    amplitude,
    angle,
    positions,
    offsets,
    tiles,
    taps_real,
    taps_imag,
    taps,
    rings_held,
    passed_out,
    field_out,
    beams,
    own,
    other,
    sent,
    masked,
    arrived1,
    summed1,
    arrived2,
    summed2,
    arrived3,
    after_in,
    before_in,
    kept,
    rings,
    factor0,
    factor1,
    beam_taps,
    phase,
    incident,
    field,
    passed,
    load_sem,
    swap_send,
    swap_recv,
    send_sem,
    recv_sem,
    edge_send,
    edge_recv,
    beam_send,
    beam_recv,
    store_sem,
):
    me, block = lax.axis_index("beam"), lax.axis_index("row")
    core = me % 2
    x, y, z = me // 2 % 4, me // 8 % 4, me // 32
    half = STRIPS // 2
    rows = tiles.shape[1]
    piece = rows // 4
    probe_id = block * lax.axis_size("beam") + me
    row_start = block * rows
    probe_row = positions[0, probe_id] - row_start
    probe_column = positions[1, probe_id]

    def at(x, y, z, core):
        return ((z * 4 + y) * 4 + x) * 2 + core

    twin = at(x, y, z, 1 - core)
    facing = at(x, y, 1 - z, core)
    along_x = [at((x + k) % 4, y, z, core) for k in (1, 2, 3)]
    along_y = [at(x, (y + k) % 4, z, core) for k in (1, 2, 3)]
    place1 = x * (1 - core) + y * core
    place2 = y * (1 - core) + x * core
    line1 = [at((x + k * (1 - core)) % 4, (y + k * core) % 4, z, core) for k in (1, 2, 3)]
    line2 = [at((x + k * core) % 4, (y + k * (1 - core)) % 4, z, core) for k in (1, 2, 3)]

    loads = []
    for strip in range(half):
        for group, target in enumerate((own, sent)):
            side = core if group == 0 else 1 - core
            column = pl.multiple_of((side * half + strip) * LANES, LANES)
            loads.append(
                pltpu.make_async_copy(
                    tiles.at[0, :, pl.ds(column, LANES)],
                    target.at[strip],
                    load_sem.at[group * half + strip],
                )
            )
    loads.append(pltpu.make_async_copy(rings_held, rings, load_sem.at[STRIPS]))
    for load in loads:
        load.start()

    barrier = pltpu.get_barrier_semaphore()
    partners = [(twin, block), (facing, block), (me, 1 - block), (facing, 1 - block)]
    partners += [(b, block) for b in along_x + along_y]
    for partner in partners:
        pl.semaphore_signal(barrier, inc=1, device_id=partner, device_id_type=MESH)

    lane = lax.broadcasted_iota(jnp.int32, (1, 1, LANES), 2)
    payload = jnp.zeros((1, 1, LANES), F32)
    for beam in range(2):
        values = (
            tilts[beam, 0].astype(F32),
            tilts[beam, 1].astype(F32),
            amplitude[beam],
            angle[beam],
        )
        for n, value in enumerate(values):
            payload = jnp.where(lane == 4 * beam + n, value, payload)
    beams[pl.ds(me, 1)] = payload

    for beam in range(2):
        tilt_row, tilt_column = tilts[beam, 0], tilts[beam, 1]
        pc, ps = phasor(tilt_row * lax.broadcasted_iota(jnp.int32, (8, BLOCK_IN), 1))
        pc, ps = pc[:1], ps[:1]
        real = taps_real[...] * pc - taps_imag[...] * ps
        imag = taps_real[...] * ps + taps_imag[...] * pc
        low = 2 * BLOCK * beam
        beam_taps[low : low + BLOCK, :] = jnp.concatenate([real, -imag], axis=1).astype(BF16)
        low += BLOCK
        beam_taps[low : low + BLOCK, :] = jnp.concatenate([imag, real], axis=1).astype(BF16)
        starts = row_start - BEFORE + BLOCK * lax.broadcasted_iota(jnp.int32, (8, NPIX), 0)
        pc, ps = phasor(
            tilt_row * starts + tilt_column * lax.broadcasted_iota(jnp.int32, (8, NPIX), 1)
        )
        phase[beam, 0] = pc
        phase[beam, 1] = ps

    pl.semaphore_wait(barrier, len(partners))
    started = []

    def copy_of(source, target, send_at, recv_at, device):
        return pltpu.make_async_remote_copy(
            src_ref=source,
            dst_ref=target,
            send_sem=send_at,
            recv_sem=recv_at,
            device_id=device,
            device_id_type=MESH,
        )

    def send(*args):
        copy = copy_of(*args)
        copy.start()
        started.append(copy)
        return copy

    def beam_chunk(size):
        return beams.at[pl.ds(pl.multiple_of(me // size * size, size), size)]

    chunk = beam_chunk(1)
    beam_copies = [send(chunk, chunk, beam_send.at[0], beam_recv.at[0], (twin, block))]
    for load in loads[:STRIPS]:
        load.wait()
    swap = send(sent, other, swap_send.at[0], swap_recv.at[0], (twin, block))

    def beam_step(size, devices, slot):
        for copy in beam_copies:
            copy.wait_recv()
        chunk = beam_chunk(size)
        beam_copies[:] = [
            send(chunk, chunk, beam_send.at[slot + k], beam_recv.at[slot + k], (device, block))
            for k, device in enumerate(devices)
        ]

    beam_step(2, along_x, 1)
    swap.wait_recv()

    copies = [None, None]
    for s in range(2):
        keep_own = jnp.where(owners[s] == me, 1.0, 0.0)
        keep_other = jnp.where(owners[s] == twin, 1.0, 0.0)
        for strip in range(half):
            value = own[strip].astype(F32) * keep_own + other[strip].astype(F32) * keep_other
            masked[s, strip] = value.astype(BF16)
        copies[s] = [
            send(
                masked.at[s, (place1 + k + 1) % 4],
                arrived1.at[s, k],
                send_sem.at[s, k],
                recv_sem.at[s, k],
                (line1[k], block),
            )
            for k in range(3)
        ]
    beam_step(8, along_y, 4)
    for s in range(2):
        for copy in copies[s]:
            copy.wait_recv()
        total = masked[s, place1].astype(F32)
        for k in range(3):
            total += arrived1[s, k].astype(F32)
        summed1[s] = total.astype(BF16)
        copies[s] = [
            send(
                summed1.at[s, pl.ds(pl.multiple_of((place2 + k + 1) % 4 * piece, piece), piece)],
                arrived2.at[s, k],
                send_sem.at[s, k + 3],
                recv_sem.at[s, k + 3],
                (line2[k], block),
            )
            for k in range(3)
        ]
    beam_step(32, [facing], 7)

    edge_to = [(me, 1 - block), (facing, 1 - block)]
    edges = [
        (0, pl.ds(0, AFTER), after_in, pl.ds(BEFORE + rows, AFTER)),
        (3, pl.ds(piece - BEFORE, BEFORE), before_in, pl.ds(0, BEFORE)),
    ]

    def edge_copies(s, n):
        _, source, target, _ = edges[n]
        return [
            copy_of(
                summed2.at[s, source],
                target.at[s, k],
                edge_send.at[s, n, k],
                edge_recv.at[s, n, k],
                edge_to[k],
            )
            for k in range(2)
        ]

    def edge_spread(s, n, peers=range(3)):
        place = kept.at[s, strip, edges[n][3]]
        return [
            copy_of(
                place, place, edge_send.at[s, n, k + 2], edge_recv.at[s, n, 2], (line2[k], block)
            )
            for k in peers
        ]

    mine = pl.ds(pl.multiple_of(place2 * piece, piece), piece)
    mine_kept = pl.ds(pl.multiple_of(place2 * piece + BEFORE, BEFORE), piece)
    strip = core * half + place1
    for s in range(2):
        for copy in copies[s]:
            copy.wait_recv()
        total = summed1[s, mine].astype(F32)
        for k in range(3):
            total += arrived2[s, k].astype(F32)
        summed2[s] = total.astype(BF16)
        copies[s] = [
            send(
                summed2.at[s],
                arrived3.at[s],
                send_sem.at[s, 6],
                recv_sem.at[s, 6],
                (facing, block),
            )
        ]
        for n in range(2):

            @pl.when(place2 == edges[n][0])
            def _(s=s, n=n):
                for copy in edge_copies(s, n):
                    copy.start()

    def back_along_second(s):
        copies[s][0].wait_recv()
        kept[s, strip, mine_kept] = (
            summed2[s].astype(F32) + arrived3[s].astype(F32)
        ).astype(BF16)
        place = kept.at[s, strip, mine_kept]
        copies[s] = [
            send(place, place, send_sem.at[s, k + 7], recv_sem.at[s, k + 7], (line2[k], block))
            for k in range(3)
        ]
        for n in range(2):

            @pl.when(place2 == edges[n][0])
            def _(n=n):
                for copy in edge_copies(s, n):
                    copy.wait_recv()
                arrived = edges[n][2]
                total = arrived[s, 0].astype(F32) + arrived[s, 1].astype(F32)
                kept[s, strip, edges[n][3]] = total.astype(BF16)
                for copy in edge_spread(s, n):
                    copy.start()

    def back_along_first(s):
        for copy in copies[s]:
            copy.wait_recv()
        for n in range(2):

            @pl.when(place2 != edges[n][0])
            def _(n=n):
                edge_spread(s, n, [0])[0].wait_recv()

        place = kept.at[s, strip]
        copies[s] = [
            send(place, place, send_sem.at[s, k + 10], recv_sem.at[s, k + 10], (line1[k], block))
            for k in range(3)
        ]

    def back_to_twin(s):
        for copy in copies[s]:
            copy.wait_recv()
        place = kept.at[s, pl.ds(pl.multiple_of(core * half, half), half)]
        copies[s] = [send(place, place, send_sem.at[s, 13], recv_sem.at[s, 13], (twin, block))]

    back_along_second(0)
    back_along_second(1)
    back_along_first(0)

    for copy in beam_copies:
        copy.wait_recv()
    reach = BLOCK_IN - 4 * RAD
    table = beams[...].reshape(beams.shape[0], LANES)
    both = jnp.concatenate([table[:, 0:4], table[:, 4:8]], axis=0)
    count = both.shape[0]
    ids = lax.broadcasted_iota(jnp.int32, (count, 1), 0)
    ids = jnp.where(ids < count // 2, 2 * ids, 2 * ids - count + 1)
    ky = both[:, 0:1].astype(jnp.int32)
    kx = both[:, 1:2].astype(jnp.int32)
    inside = (((ids - offsets[probe_id] + count) & (count - 1)) < count // 2).astype(F32)
    weight = both[:, 2:3] * inside * (1.0 / math.sqrt(count // 2))
    angle_c, angle_s = circle(both[:, 3:4] * (0.5 / math.pi))
    rel = lax.broadcasted_iota(jnp.int32, (count, LANES), 1) - BEFORE
    pc, ps = phasor(ky * rel - kx * probe_column)
    left_real = weight * (angle_c * pc - angle_s * ps)
    left_imag = weight * (angle_s * pc + angle_c * ps)
    left_real, left_imag = left_real.T[:reach], left_imag.T[:reach]
    left = jnp.concatenate(
        [
            jnp.concatenate([left_real, -left_imag], axis=1),
            jnp.concatenate([left_imag, left_real], axis=1),
        ],
        axis=0,
    )
    high = left.astype(BF16)
    left = jnp.concatenate([high, (left - high.astype(F32)).astype(BF16)], axis=0)
    pc, ps = phasor(kx * lax.broadcasted_iota(jnp.int32, (count, LANES), 1))
    qc, qs = phasor(kx * (LANES * lax.broadcasted_iota(jnp.int32, (count, STRIPS), 1)))
    for pair in range(STRIPS // 2):
        right = []
        for n in (2 * pair, 2 * pair + 1):
            c, s = qc[:, n : n + 1], qs[:, n : n + 1]
            right.append(jnp.concatenate([pc * c - ps * s, pc * s + ps * c], axis=0).astype(BF16))
        wave = dot(left, jnp.concatenate(right, axis=1))
        columns = slice(pair * 2 * LANES, (pair + 1) * 2 * LANES)
        incident[:, columns] = wave[: 2 * reach] + wave[2 * reach :]

    back_along_first(1)
    back_to_twin(0)

    def window(s, first, count, pair):
        chosen = lax.broadcasted_iota(jnp.int32, (count, KEPT), 0) + first
        chosen = (lax.broadcasted_iota(jnp.int32, (count, KEPT), 1) == chosen).astype(BF16)
        held = jnp.concatenate([kept[s, 2 * pair], kept[s, 2 * pair + 1]], axis=1)
        c, s = cos_sin(dot(chosen, held))
        return c.astype(BF16).astype(F32), s.astype(BF16).astype(F32)

    copies[0][0].wait_recv()

    def factors0(step, carry):
        held = pl.ds(pl.multiple_of(step * STEP, 16), STEP)
        for strip in range(STRIPS):
            columns = slice(strip * LANES, (strip + 1) * LANES)
            c, s = cos_sin(kept[0, strip, held, :].astype(F32))
            factor0[0, held, columns] = c.astype(BF16)
            factor0[1, held, columns] = s.astype(BF16)
        return carry

    lax.fori_loop(0, factor0.shape[1] // STEP, factors0, 0)
    back_to_twin(1)
    field[...] = jnp.zeros(field.shape, BF16)
    for pair in range(STRIPS // 2):
        columns = slice(pair * QUARTER, (pair + 1) * QUARTER)
        fr, fi = window(0, probe_row, reach, pair)
        r, i = incident[:reach, columns], incident[reach:, columns]
        field[:reach, columns] = (r * fr - i * fi).astype(BF16)
        field[BLOCK_IN : BLOCK_IN + reach, columns] = (r * fi + i * fr).astype(BF16)

    copies[1][0].wait_recv()

    def factors1(step, carry):
        start = pl.multiple_of(step * STEP, 16)
        for strip in range(STRIPS):
            columns = slice(strip * LANES, (strip + 1) * LANES)
            values = kept[1, strip, pl.ds(start, STEP + 16), :].astype(F32)[RAD : RAD + STEP]
            c, s = cos_sin(values)
            factor1[0, pl.ds(start, STEP), columns] = c.astype(BF16)
            factor1[1, pl.ds(start, STEP), columns] = s.astype(BF16)
        return carry

    lax.fori_loop(0, factor1.shape[1] // STEP, factors1, 0)
    loads[STRIPS].wait()

    def turned(mixed, count, beam, block):
        real, imag = mixed[:count], mixed[count:]
        pc = phase[beam, 0, pl.ds(block, 1), :]
        ps = phase[beam, 1, pl.ds(block, 1), :]
        return split(real * pc - imag * ps, real * ps + imag * pc)

    def pass_on(quarters, start, count):
        for q, (real, imag) in enumerate(quarters):
            columns = slice(q * QUARTER, (q + 1) * QUARTER)
            fr = factor1[0, pl.ds(start, count), columns].astype(F32)
            fi = factor1[1, pl.ds(start, count), columns].astype(F32)
            for beam in range(2):
                r, i = real[beam * count : (beam + 1) * count], imag[beam * count : (beam + 1) * count]
                passed[beam, 0, pl.ds(start, count), columns] = (r * fr - i * fi).astype(BF16)
                passed[beam, 1, pl.ds(start, count), columns] = (r * fi + i * fr).astype(BF16)

    def store(n, start, count):
        part = pl.ds(start, count)
        return pltpu.make_async_copy(
            passed.at[:, :, part], passed_out.at[:, :, part], store_sem.at[n]
        )

    def block_of(start):
        return jnp.concatenate(
            [factor0[0, pl.ds(start, BLOCK_IN), :], factor0[1, pl.ds(start, BLOCK_IN), :]], axis=0
        )

    def first_block(block, carry):
        start = pl.multiple_of(block * BLOCK, 16)
        mixed = dot(beam_taps[...], block_of(start))
        parts = [
            turned(mixed[2 * BLOCK * beam : 2 * BLOCK * (beam + 1)], BLOCK, beam, block)
            for beam in range(2)
        ]
        pass_on(propagate(parts, rings), start, BLOCK)
        store(block, start, BLOCK).start()
        return carry

    lax.fori_loop(0, FULL_BLOCKS, first_block, 0, unroll=2)

    out = PASSED - TAIL
    tops = [BLOCK * n for n in range(4)]
    left = jnp.concatenate([beam_taps[top : top + out] for top in tops])
    mixed = dot(left, block_of(TAIL))
    parts = [
        turned(mixed[2 * out * beam : 2 * out * (beam + 1)], out, beam, FULL_BLOCKS)
        for beam in range(2)
    ]
    mixed = dot(jnp.concatenate([taps[:out], taps[BLOCK : BLOCK + out]]), field[...])
    parts.append(split(mixed[:out], mixed[out:]))
    quarters = propagate(parts, rings)
    pass_on(quarters, TAIL, out)
    last = store(FULL_BLOCKS, TAIL, out)
    last.start()
    field[...] = jnp.zeros(field.shape, BF16)
    for pair, (real, imag) in enumerate(quarters):
        columns = slice(pair * QUARTER, (pair + 1) * QUARTER)
        r, i = real[2 * out :], imag[2 * out :]
        fr, fi = window(1, probe_row + RAD, out, pair)
        field[:out, columns] = (r * fr - i * fi).astype(BF16)
        field[BLOCK_IN : BLOCK_IN + out, columns] = (r * fi + i * fr).astype(BF16)
    field_copy = pltpu.make_async_copy(field, field_out, store_sem.at[FULL_BLOCKS + 1])
    field_copy.start()

    for copy in started:
        copy.wait_send()
    for s in range(2):
        for n in range(2):

            @pl.when(place2 == edges[n][0])
            def _(s=s, n=n):
                for copy in edge_copies(s, n) + edge_spread(s, n):
                    copy.wait_send()

    for n in range(FULL_BLOCKS):
        store(n, n * BLOCK, BLOCK).wait()
    last.wait()
    field_copy.wait()


def first_slice(owners, tilts, amplitude, angle, positions, offsets, tiles):
    real, imag = row_matrices()
    taps = np.block([[real, -imag], [imag, real]]).astype(ml_dtypes.bfloat16)
    half = STRIPS // 2
    rows = tiles.shape[1]
    piece = rows // 4
    vmem = pl.BlockSpec(memory_space=pltpu.VMEM)
    smem = pl.BlockSpec(memory_space=pltpu.SMEM)
    anywhere = pl.BlockSpec(memory_space=pl.ANY)
    reach = BLOCK_IN - 4 * RAD
    return pl.pallas_call(
        first_kernel,
        out_shape=(
            jax.ShapeDtypeStruct((2, 2, PASSED, NPIX), BF16),
            jax.ShapeDtypeStruct((2 * BLOCK_IN, NPIX), BF16),
        ),
        in_specs=[smem] * 6 + [anywhere] + [vmem] * 3 + [anywhere],
        out_specs=(anywhere, anywhere),
        scratch_shapes=[
            pltpu.VMEM((lax.axis_size("beam"), 1, LANES), F32),
            pltpu.VMEM((half, rows, LANES), BF16),
            pltpu.VMEM((half, rows, LANES), BF16),
            pltpu.VMEM((half, rows, LANES), BF16),
            pltpu.VMEM((2, half, rows, LANES), BF16),
            pltpu.VMEM((2, 3, rows, LANES), BF16),
            pltpu.VMEM((2, rows, LANES), BF16),
            pltpu.VMEM((2, 3, piece, LANES), BF16),
            pltpu.VMEM((2, piece, LANES), BF16),
            pltpu.VMEM((2, piece, LANES), BF16),
            pltpu.VMEM((2, 2, AFTER, LANES), BF16),
            pltpu.VMEM((2, 2, BEFORE, LANES), BF16),
            pltpu.VMEM((2, STRIPS, KEPT, LANES), BF16),
            pltpu.VMEM((4, 2 * QUARTER, 2 * QUARTER), BF16),
            pltpu.VMEM((2, TAIL + BLOCK_IN, NPIX), BF16),
            pltpu.VMEM((2, PASSED, NPIX), BF16),
            pltpu.VMEM((4 * BLOCK, 2 * BLOCK_IN), BF16),
            pltpu.VMEM((2, 2, 8, NPIX), F32),
            pltpu.VMEM((2 * reach, NPIX), F32),
            pltpu.VMEM((2 * BLOCK_IN, NPIX), BF16),
            pltpu.VMEM((2, 2, PASSED, NPIX), BF16),
            pltpu.SemaphoreType.DMA((STRIPS + 1,)),
            pltpu.SemaphoreType.DMA((1,)),
            pltpu.SemaphoreType.DMA((1,)),
            pltpu.SemaphoreType.DMA((2, 14)),
            pltpu.SemaphoreType.DMA((2, 14)),
            pltpu.SemaphoreType.DMA((2, 2, 5)),
            pltpu.SemaphoreType.DMA((2, 2, 3)),
            pltpu.SemaphoreType.DMA((8,)),
            pltpu.SemaphoreType.DMA((8,)),
            pltpu.SemaphoreType.DMA((FULL_BLOCKS + 2,)),
        ],
        compiler_params=pltpu.CompilerParams(
            collective_id=0, has_side_effects=True, vmem_limit_bytes=60 * 2**20
        ),
        name="first_slice",
    )(
        owners,
        tilts,
        amplitude,
        angle,
        positions,
        offsets,
        tiles,
        jnp.asarray(real),
        jnp.asarray(imag),
        jnp.asarray(taps),
        jnp.asarray(ring_matrices()),
    )


def second_kernel(
    positions, taps, rings, passed_in, field, exit_out, probe, passed, waves, load_sem, store_sem
):
    probe_id = lax.axis_index("row") * lax.axis_size("beam") + lax.axis_index("beam")
    loads = []
    end = 0
    for n in range(FULL_BLOCKS + 1):
        start, end = end, min(n * BLOCK + BLOCK_IN, PASSED)
        loads.append(
            pltpu.make_async_copy(
                passed_in.at[:, :, start:end], passed.at[:, :, start:end], load_sem.at[n]
            )
        )
        loads[n].start()
    spare = passed.shape[2] - PASSED
    passed[:, :, PASSED:, :] = jnp.zeros((2, 2, spare, NPIX), BF16)

    def block_of(beam, start):
        return jnp.concatenate(
            [passed[beam, 0, start : start + BLOCK_IN], passed[beam, 1, start : start + BLOCK_IN]],
            axis=0,
        )

    stores = []

    def write(quarters, start, count):
        for q, (real, imag) in enumerate(quarters):
            for beam in range(2):
                chosen = slice(beam * count, (beam + 1) * count)
                low = q * QUARTER
                waves[beam, start : start + count, low : low + QUARTER] = real[chosen].astype(BF16)
                low += NPIX
                waves[beam, start : start + count, low : low + QUARTER] = imag[chosen].astype(BF16)
        part = slice(start, start + count)
        stores.append(
            pltpu.make_async_copy(
                waves.at[:, part], exit_out.at[:, part], store_sem.at[len(stores)]
            )
        )
        stores[-1].start()

    for block in range(FULL_BLOCKS):
        loads[block].wait()
        start = block * BLOCK
        parts = []
        for beam in range(2):
            mixed = dot(taps[...], block_of(beam, start))
            parts.append(split(mixed[:BLOCK], mixed[BLOCK:]))
        write(propagate(parts, rings), start, BLOCK)

    loads[FULL_BLOCKS].wait()
    left = jnp.concatenate([taps[:WIN], taps[BLOCK : BLOCK + WIN]])
    parts = []
    for mixed in [dot(left, block_of(beam, TAIL)) for beam in range(2)] + [dot(left, field[...])]:
        parts.append(split(mixed[:WIN], mixed[WIN:]))
    quarters = propagate(parts, rings)
    write(quarters, TAIL, WIN)
    shift = (NPIX - positions[1, probe_id]) & (NPIX - 1)
    real = jnp.concatenate([real[2 * WIN :] for real, _ in quarters], axis=1)
    imag = jnp.concatenate([imag[2 * WIN :] for _, imag in quarters], axis=1)
    real = pltpu.roll(real, shift, 1)[:, :WIN]
    imag = pltpu.roll(imag, shift, 1)[:, :WIN]
    probe[0, 0] = jnp.concatenate([real, imag], axis=1)
    for copy in stores:
        copy.wait()


def second_slice(positions, passed, field):
    real, imag = row_matrices()
    taps = np.block([[real, -imag], [imag, real]]).astype(ml_dtypes.bfloat16)
    vmem = pl.BlockSpec(memory_space=pltpu.VMEM)
    smem = pl.BlockSpec(memory_space=pltpu.SMEM)
    anywhere = pl.BlockSpec(memory_space=pl.ANY)
    return pl.pallas_call(
        second_kernel,
        out_shape=(
            jax.ShapeDtypeStruct((2, NPIX // 2, 2 * NPIX), BF16),
            jax.ShapeDtypeStruct((1, 1, WIN, 2 * WIN), F32),
        ),
        in_specs=[smem, vmem, vmem, anywhere, vmem],
        out_specs=(anywhere, vmem),
        scratch_shapes=[
            pltpu.VMEM((2, 2, TAIL + BLOCK_IN, NPIX), BF16),
            pltpu.VMEM((2, NPIX // 2, 2 * NPIX), BF16),
            pltpu.SemaphoreType.DMA((FULL_BLOCKS + 1,)),
            pltpu.SemaphoreType.DMA((FULL_BLOCKS + 1,)),
        ],
        compiler_params=pltpu.CompilerParams(vmem_limit_bytes=60 * 2**20),
        name="second_slice",
    )(positions, jnp.asarray(taps), jnp.asarray(ring_matrices()), passed, field)


def body(tilts, potentials, owners, beam_amplitude, beam_phase, probe_positions, beam_offsets):
    positions = probe_positions.T
    passed, field = first_slice(
        owners, tilts, beam_amplitude, beam_phase, positions, beam_offsets, potentials
    )
    return second_slice(positions, passed, field)


def solution(mesh):
    return jax.shard_map(
        body,
        mesh=mesh,
        in_specs=(P("beam", None), P("beam", "row", None), P(), P("beam"), P("beam"), P(), P()),
        out_specs=(P("beam", "row", None), P("row", "beam", None, None)),
        check_vma=False,
    )
```

time: 2130 us -> 60.7 us (0.03); the launches traced: 2100 us -> 60.5 us
  local copies, waits for them, and re-layouts: 955 us -> 0 us
  waiting for transfers between devices: 913 us -> 0 us
  other arithmetic: 168 us -> 0 us
  Pallas kernels: 0 us -> 59.9 us
  matrix products: 43.5 us -> 0 us
    gather x1024 -> x0, local copies, waits for them, and re-layouts: 925 us -> none
    psum x1 -> x0, waiting for transfers between devices: 562 us -> none  [spread_2(): return lax.psum(kept, axis)]
    reduce_scatter x2 -> x0, waiting for transfers between devices: 340 us -> none  [the longest x1 280 us: body(): lax.psum_scatter(lax.slice_in_dim(folded, 0, lax.axis_size('beam') * prob...]
    another operation x5 -> x0, other arithmetic: 137 us -> none
    pallas_call x0 -> x2, Pallas kernels: none -> 59.9 us  [the longest x1 50.3 us: first_slice(): pl.pallas_call(first_kernel, out_shape=(jax.ShapeDtypeStruct((2, 2, PASSE...]
    dot_general x6 -> x0, matrix products: 43.5 us -> none  [the longest x2 22.7 us: body(): jnp.einsum('brk,kl->brl', transmitted, matrix, preferred_element_type=jnp...]
  transfers between devices with their start and end apart: 7 -> 0, of which waited for: 7 -> 0; matrix products, arithmetic and copies ran while one was open for 0% -> 0% of each run, Pallas kernels for 0% -> 0%
where the time goes in v1:
time: 60.7 us; the launch traced here: 60.5 us
  Pallas kernels  59.9 us (99%)
  between operations  0.64 us (1%)
    pallas_call x1, Pallas kernels, first_slice(): pl.pallas_call(first_kernel, out_shape=(jax.ShapeDtypeStruct((2, 2, PASSE...  50.3 us
    pallas_call x1, Pallas kernels, second_slice(): pl.pallas_call(second_kernel, out_shape=(jax.ShapeDtypeStruct((2, NPIX //...  9.57 us

profile of v1, /device:TPU:1, one launch (start us, length us, event | category | flops | bytes accessed | tf_op | source)
XLA Modules:
  0.0 60.5 jit_solution(16367915414506192229)
XLA Ops:
  0.6 50.3 %first_slice.1 = (bf16[2,2,528,1024]{3,2,1,0:T(8,128)(2,1)}, bf16[256,1024]{1,0:T(8,128)(2,1)}) custom-call(s32[2]{0:T(128)} %owners.1, s32[2,2]{1,0:T(2,128)} %tilts.1, f32[2]{0:T(128)} %amplitude.1, f32[2]{0:T(128)} %angle.1, s32[2,128]{1,0:T(2,128)} %bitcast.1, s32[128]{0:T(128)} %offsets.1, bf16[1,512,1024]{2,1,0:T(8,128)(2,1)} %tiles.1, ...), custom_call_target="tpu_custom_call" | custom-call | tf_op jit(solution)/shard_map/first_slice/pallas_call | solution.py:610
  51.0 9.6 %second_slice.1 = (bf16[2,512,2048]{2,1,0:T(8,128)(2,1)}, f32[1,1,64,128]{3,2,1,0:T(8,128)}) custom-call(s32[2,128]{1,0:T(2,128)} %bitcast.2, bf16[224,256]{1,0:T(8,128)(2,1)} %constant.10.clone.taps, bf16[4,512,512]{2,1,0:T(8,128)(2,1)} %constant.11.clone.rings_held.rings, bf16[2,2,528,1024]{3,2,1,0:T(8,128)(2,1)} %get-tuple-element.4.passed_in, ...), custom_call_target="tpu_custom_call" | custom-call | tf_op jit(solution)/shard_map/second_slice/pallas_call | solution.py:743

commit v2 on v1

--- a/solution.py
+++ b/solution.py
@@ -13,7 +13,8 @@
 RAD = 8
 WIN = 64
 ROW_CHIRP = 0.07
-QUARTER = NPIX // 4
+RINGS = 8
+QUARTER = NPIX // RINGS
 LANES = 128
 STRIPS = NPIX // LANES
 BEFORE = 2 * RAD
@@ -59,12 +60,12 @@
     kernel = (spectrum @ np.exp(1j * turns)) / NPIX
     held_real = kernel.real.astype(np.float32).astype(ml_dtypes.bfloat16).astype(np.float64)
     held_imag = kernel.imag.astype(np.float32).astype(ml_dtypes.bfloat16).astype(np.float64)
-    quarters = (held_real + 1j * held_imag).reshape(4, QUARTER)
+    quarters = (held_real + 1j * held_imag).reshape(RINGS, QUARTER)
     steps = np.arange(QUARTER)[None, :] - np.arange(QUARTER)[:, None]
     matrices = []
-    for ring in range(4):
-        root = 1j**ring
-        folded = sum(root**part * quarters[part] for part in range(4)) / 4.0
+    for ring in range(RINGS):
+        root = np.exp(2j * np.pi * ring / RINGS)
+        folded = sum(root**part * quarters[part] for part in range(RINGS)) / RINGS
         matrix = np.where(steps >= 0, 1.0, root) * folded[steps % QUARTER]
         matrices.append(
             np.block([[matrix.real, matrix.imag], [-matrix.imag, matrix.real]]).astype(np.float32)
@@ -85,7 +86,7 @@
     return total
 
 
-EVEN = fitted(np.cos, (0, 2, 4, 6, 8))
+EVEN = fitted(np.cos, (0, 2, 4, 6))
 ODD = fitted(np.sin, (1, 3, 5, 7))
 TURN_EVEN = fitted(lambda u: np.cos(2 * np.pi * u), range(0, 17, 2), 0.5)
 TURN_ODD = fitted(lambda u: np.sin(2 * np.pi * u), range(1, 18, 2), 0.5)
@@ -113,21 +114,58 @@
     return jnp.dot(a, b, preferred_element_type=F32)
 
 
+HALF = math.sqrt(0.5)
+
+
+def add(a, b):
+    return a[0] + b[0], a[1] + b[1]
+
+
+def less(a, b):
+    return a[0] - b[0], a[1] - b[1]
+
+
+def plus_i(a, b):
+    return a[0] - b[1], a[1] + b[0]
+
+
+def less_i(a, b):
+    return a[0] + b[1], a[1] - b[0]
+
+
 def split(real, imag):
-    r = [real[:, q * QUARTER : (q + 1) * QUARTER] for q in range(4)]
-    i = [imag[:, q * QUARTER : (q + 1) * QUARTER] for q in range(4)]
-    ar, ai, br, bi = r[0] + r[2], i[0] + i[2], r[0] - r[2], i[0] - i[2]
-    cr, ci, dr, di = r[1] + r[3], i[1] + i[3], r[1] - r[3], i[1] - i[3]
-    pairs = ((ar + cr, ai + ci), (br - di, bi + dr), (ar - cr, ai - ci), (br + di, bi - dr))
-    return [jnp.concatenate([p.astype(BF16), q.astype(BF16)], axis=1) for p, q in pairs]
+    x = [
+        tuple(f[:, q * QUARTER : (q + 1) * QUARTER] for f in (real, imag)) for q in range(RINGS)
+    ]
+    rings = [None] * RINGS
+    for odd in range(2):
+        a = [(less if odd else add)(x[q], x[q + 4]) for q in range(4)]
+        if odd:
+            a[1] = ((a[1][0] - a[1][1]) * HALF, (a[1][0] + a[1][1]) * HALF)
+            a[3] = ((a[3][0] + a[3][1]) * -HALF, (a[3][0] - a[3][1]) * HALF)
+            b, c = plus_i(a[0], a[2]), add(a[1], a[3])
+            e, d = less_i(a[0], a[2]), less(a[1], a[3])
+        else:
+            b, c = add(a[0], a[2]), add(a[1], a[3])
+            e, d = less(a[0], a[2]), less(a[1], a[3])
+        rings[odd], rings[4 + odd] = add(b, c), less(b, c)
+        rings[2 + odd], rings[6 + odd] = plus_i(e, d), less_i(e, d)
+    return [jnp.concatenate([p.astype(BF16), q.astype(BF16)], axis=1) for p, q in rings]
 
 
 def join(products):
-    r = [p[:, :QUARTER] for p in products]
-    i = [p[:, QUARTER:] for p in products]
-    ar, ai, br, bi = r[0] + r[2], i[0] + i[2], r[0] - r[2], i[0] - i[2]
-    cr, ci, dr, di = r[1] + r[3], i[1] + i[3], r[1] - r[3], i[1] - i[3]
-    return ((ar + cr, ai + ci), (br + di, bi - dr), (ar - cr, ai - ci), (br - di, bi + dr))
+    y = [(p[:, :QUARTER], p[:, QUARTER:]) for p in products]
+    halves = []
+    for odd in range(2):
+        b, e = add(y[odd], y[4 + odd]), less(y[odd], y[4 + odd])
+        c, d = add(y[2 + odd], y[6 + odd]), less(y[2 + odd], y[6 + odd])
+        halves.append([add(b, c), less_i(e, d), less(b, c), plus_i(e, d)])
+    even, o = halves
+    o[1] = ((o[1][0] + o[1][1]) * HALF, (o[1][1] - o[1][0]) * HALF)
+    o[3] = ((o[3][1] - o[3][0]) * HALF, (o[3][0] + o[3][1]) * -HALF)
+    first = [add(even[0], o[0]), add(even[1], o[1]), less_i(even[2], o[2]), add(even[3], o[3])]
+    last = [less(even[0], o[0]), less(even[1], o[1]), plus_i(even[2], o[2]), less(even[3], o[3])]
+    return first + last
 
 
 def propagate(parts, rings):
@@ -144,7 +182,7 @@
     tiles,
     taps_real,
     taps_imag,
-    taps,
+    taps_held,
     rings_held,
     passed_out,
     field_out,
@@ -161,6 +199,7 @@
     after_in,
     before_in,
     kept,
+    taps,
     rings,
     factor0,
     factor1,
@@ -174,6 +213,8 @@
     swap_recv,
     send_sem,
     recv_sem,
+    twin_send,
+    twin_recv,
     edge_send,
     edge_recv,
     beam_send,
@@ -203,10 +244,16 @@
     line1 = [at((x + k * (1 - core)) % 4, (y + k * core) % 4, z, core) for k in (1, 2, 3)]
     line2 = [at((x + k * core) % 4, (y + k * (1 - core)) % 4, z, core) for k in (1, 2, 3)]
 
+    barrier = pltpu.get_barrier_semaphore()
+    partners = [(twin, block), (facing, block), (me, 1 - block), (facing, 1 - block)]
+    partners += [(b, block) for b in along_x + along_y]
+    for partner in partners:
+        pl.semaphore_signal(barrier, inc=1, device_id=partner, device_id_type=MESH)
+
     loads = []
-    for strip in range(half):
-        for group, target in enumerate((own, sent)):
-            side = core if group == 0 else 1 - core
+    for group, target in enumerate((sent, own)):
+        for strip in range(half):
+            side = 1 - core if group == 0 else core
             column = pl.multiple_of((side * half + strip) * LANES, LANES)
             loads.append(
                 pltpu.make_async_copy(
@@ -216,14 +263,9 @@
                 )
             )
     loads.append(pltpu.make_async_copy(rings_held, rings, load_sem.at[STRIPS]))
-    for load in loads:
+    loads.append(pltpu.make_async_copy(taps_held, taps, load_sem.at[STRIPS + 1]))
+    for load in loads[:STRIPS]:
         load.start()
-
-    barrier = pltpu.get_barrier_semaphore()
-    partners = [(twin, block), (facing, block), (me, 1 - block), (facing, 1 - block)]
-    partners += [(b, block) for b in along_x + along_y]
-    for partner in partners:
-        pl.semaphore_signal(barrier, inc=1, device_id=partner, device_id_type=MESH)
 
     lane = lax.broadcasted_iota(jnp.int32, (1, 1, LANES), 2)
     payload = jnp.zeros((1, 1, LANES), F32)
@@ -279,9 +321,22 @@
 
     chunk = beam_chunk(1)
     beam_copies = [send(chunk, chunk, beam_send.at[0], beam_recv.at[0], (twin, block))]
-    for load in loads[:STRIPS]:
+    swaps = []
+    for strip in range(half):
+        loads[strip].wait()
+        swaps.append(
+            send(
+                sent.at[strip],
+                other.at[strip],
+                swap_send.at[strip],
+                swap_recv.at[strip],
+                (twin, block),
+            )
+        )
+    for load in loads[half:STRIPS]:
         load.wait()
-    swap = send(sent, other, swap_send.at[0], swap_recv.at[0], (twin, block))
+    for load in loads[STRIPS:]:
+        load.start()
 
     def beam_step(size, devices, slot):
         for copy in beam_copies:
@@ -292,11 +347,12 @@
             for k, device in enumerate(devices)
         ]
 
-    beam_step(2, along_x, 1)
-    swap.wait_recv()
+    for swap in swaps:
+        swap.wait_recv()
 
     copies = [None, None]
-    for s in range(2):
+
+    def out_along_first(s):
         keep_own = jnp.where(owners[s] == me, 1.0, 0.0)
         keep_other = jnp.where(owners[s] == twin, 1.0, 0.0)
         for strip in range(half):
@@ -312,8 +368,8 @@
             )
             for k in range(3)
         ]
-    beam_step(8, along_y, 4)
-    for s in range(2):
+
+    def out_along_second(s):
         for copy in copies[s]:
             copy.wait_recv()
         total = masked[s, place1].astype(F32)
@@ -330,7 +386,13 @@
             )
             for k in range(3)
         ]
-    beam_step(32, [facing], 7)
+
+    out_along_first(0)
+    beam_step(2, along_x, 1)
+    out_along_first(1)
+    out_along_second(0)
+    beam_step(8, along_y, 4)
+    out_along_second(1)
 
     edge_to = [(me, 1 - block), (facing, 1 - block)]
     edges = [
@@ -363,7 +425,8 @@
     mine = pl.ds(pl.multiple_of(place2 * piece, piece), piece)
     mine_kept = pl.ds(pl.multiple_of(place2 * piece + BEFORE, BEFORE), piece)
     strip = core * half + place1
-    for s in range(2):
+
+    def out_to_facing(s):
         for copy in copies[s]:
             copy.wait_recv()
         total = summed1[s, mine].astype(F32)
@@ -382,7 +445,7 @@
         for n in range(2):
 
             @pl.when(place2 == edges[n][0])
-            def _(s=s, n=n):
+            def _(n=n):
                 for copy in edge_copies(s, n):
                     copy.start()
 
@@ -408,30 +471,53 @@
                 for copy in edge_spread(s, n):
                     copy.start()
 
+        onward(s, mine_kept)
+
+    def line_copy(s, k, held, at_strip):
+        place = kept.at[s, at_strip, held]
+        return copy_of(
+            place, place, send_sem.at[s, k + 10], recv_sem.at[s, k + 10], (line1[k], block)
+        )
+
+    def onward(s, held):
+        for k in range(3):
+            line_copy(s, k, held, strip).start()
+
+    def strip_to_twin(s, n, at_strip):
+        place = kept.at[s, at_strip]
+        twin_copies[s].append(
+            send(place, place, twin_send.at[s, n], twin_recv.at[s, n], (twin, block))
+        )
+
+    twin_copies = [[], []]
+    whole = pl.ds(0, KEPT)
+
     def back_along_first(s):
-        for copy in copies[s]:
-            copy.wait_recv()
+        for k in (0, 2, 1):
+            copies[s][k].wait_recv()
+            came = (place2 + 3 - k) % 4 * piece + BEFORE
+            onward(s, pl.ds(pl.multiple_of(came, BEFORE), piece))
         for n in range(2):
 
             @pl.when(place2 != edges[n][0])
             def _(n=n):
                 edge_spread(s, n, [0])[0].wait_recv()
 
-        place = kept.at[s, strip]
-        copies[s] = [
-            send(place, place, send_sem.at[s, k + 10], recv_sem.at[s, k + 10], (line1[k], block))
-            for k in range(3)
-        ]
+            onward(s, edges[n][3])
+        strip_to_twin(s, 3, strip)
 
     def back_to_twin(s):
-        for copy in copies[s]:
-            copy.wait_recv()
-        place = kept.at[s, pl.ds(pl.multiple_of(core * half, half), half)]
-        copies[s] = [send(place, place, send_sem.at[s, 13], recv_sem.at[s, 13], (twin, block))]
-
+        for k in (0, 2, 1):
+            line_copy(s, k, whole, strip).wait_recv()
+            strip_to_twin(s, k, core * half + (place1 + 3 - k) % 4)
+
+    out_to_facing(0)
+    beam_step(32, [facing], 7)
+    out_to_facing(1)
     back_along_second(0)
     back_along_second(1)
     back_along_first(0)
+    back_along_first(1)
 
     for copy in beam_copies:
         copy.wait_recv()
@@ -471,7 +557,6 @@
         columns = slice(pair * 2 * LANES, (pair + 1) * 2 * LANES)
         incident[:, columns] = wave[: 2 * reach] + wave[2 * reach :]
 
-    back_along_first(1)
     back_to_twin(0)
 
     def window(s, first, count, pair):
@@ -481,7 +566,8 @@
         c, s = cos_sin(dot(chosen, held))
         return c.astype(BF16).astype(F32), s.astype(BF16).astype(F32)
 
-    copies[0][0].wait_recv()
+    for copy in twin_copies[0]:
+        copy.wait_recv()
 
     def factors0(step, carry):
         held = pl.ds(pl.multiple_of(step * STEP, 16), STEP)
@@ -496,13 +582,14 @@
     back_to_twin(1)
     field[...] = jnp.zeros(field.shape, BF16)
     for pair in range(STRIPS // 2):
-        columns = slice(pair * QUARTER, (pair + 1) * QUARTER)
+        columns = slice(pair * 2 * LANES, (pair + 1) * 2 * LANES)
         fr, fi = window(0, probe_row, reach, pair)
         r, i = incident[:reach, columns], incident[reach:, columns]
         field[:reach, columns] = (r * fr - i * fi).astype(BF16)
         field[BLOCK_IN : BLOCK_IN + reach, columns] = (r * fi + i * fr).astype(BF16)
 
-    copies[1][0].wait_recv()
+    for copy in twin_copies[1]:
+        copy.wait_recv()
 
     def factors1(step, carry):
         start = pl.multiple_of(step * STEP, 16)
@@ -515,7 +602,8 @@
         return carry
 
     lax.fori_loop(0, factor1.shape[1] // STEP, factors1, 0)
-    loads[STRIPS].wait()
+    for load in loads[STRIPS:]:
+        load.wait()
 
     def turned(mixed, count, beam, block):
         real, imag = mixed[:count], mixed[count:]
@@ -572,9 +660,12 @@
     last = store(FULL_BLOCKS, TAIL, out)
     last.start()
     field[...] = jnp.zeros(field.shape, BF16)
-    for pair, (real, imag) in enumerate(quarters):
-        columns = slice(pair * QUARTER, (pair + 1) * QUARTER)
-        r, i = real[2 * out :], imag[2 * out :]
+    for pair in range(STRIPS // 2):
+        columns = slice(pair * 2 * LANES, (pair + 1) * 2 * LANES)
+        r, i = [
+            jnp.concatenate([quarters[2 * pair + n][part][2 * out :] for n in range(2)], axis=1)
+            for part in range(2)
+        ]
         fr, fi = window(1, probe_row + RAD, out, pair)
         field[:out, columns] = (r * fr - i * fi).astype(BF16)
         field[BLOCK_IN : BLOCK_IN + out, columns] = (r * fi + i * fr).astype(BF16)
@@ -584,6 +675,8 @@
     for copy in started:
         copy.wait_send()
     for s in range(2):
+        for k in range(3):
+            line_copy(s, k, whole, strip).wait_send()
         for n in range(2):
 
             @pl.when(place2 == edges[n][0])
@@ -613,7 +706,7 @@
             jax.ShapeDtypeStruct((2, 2, PASSED, NPIX), BF16),
             jax.ShapeDtypeStruct((2 * BLOCK_IN, NPIX), BF16),
         ),
-        in_specs=[smem] * 6 + [anywhere] + [vmem] * 3 + [anywhere],
+        in_specs=[smem] * 6 + [anywhere] + [vmem] * 2 + [anywhere] * 2,
         out_specs=(anywhere, anywhere),
         scratch_shapes=[
             pltpu.VMEM((lax.axis_size("beam"), 1, LANES), F32),
@@ -629,7 +722,8 @@
             pltpu.VMEM((2, 2, AFTER, LANES), BF16),
             pltpu.VMEM((2, 2, BEFORE, LANES), BF16),
             pltpu.VMEM((2, STRIPS, KEPT, LANES), BF16),
-            pltpu.VMEM((4, 2 * QUARTER, 2 * QUARTER), BF16),
+            pltpu.VMEM((2 * BLOCK, 2 * BLOCK_IN), BF16),
+            pltpu.VMEM((RINGS, 2 * QUARTER, 2 * QUARTER), BF16),
             pltpu.VMEM((2, TAIL + BLOCK_IN, NPIX), BF16),
             pltpu.VMEM((2, PASSED, NPIX), BF16),
             pltpu.VMEM((4 * BLOCK, 2 * BLOCK_IN), BF16),
@@ -637,11 +731,13 @@
             pltpu.VMEM((2 * reach, NPIX), F32),
             pltpu.VMEM((2 * BLOCK_IN, NPIX), BF16),
             pltpu.VMEM((2, 2, PASSED, NPIX), BF16),
-            pltpu.SemaphoreType.DMA((STRIPS + 1,)),
-            pltpu.SemaphoreType.DMA((1,)),
-            pltpu.SemaphoreType.DMA((1,)),
-            pltpu.SemaphoreType.DMA((2, 14)),
-            pltpu.SemaphoreType.DMA((2, 14)),
+            pltpu.SemaphoreType.DMA((STRIPS + 2,)),
+            pltpu.SemaphoreType.DMA((half,)),
+            pltpu.SemaphoreType.DMA((half,)),
+            pltpu.SemaphoreType.DMA((2, 13)),
+            pltpu.SemaphoreType.DMA((2, 13)),
+            pltpu.SemaphoreType.DMA((2, 4)),
+            pltpu.SemaphoreType.DMA((2, 4)),
             pltpu.SemaphoreType.DMA((2, 2, 5)),
             pltpu.SemaphoreType.DMA((2, 2, 3)),
             pltpu.SemaphoreType.DMA((8,)),
@@ -668,10 +764,23 @@
 
 
 def second_kernel(
-    positions, taps, rings, passed_in, field, exit_out, probe, passed, waves, load_sem, store_sem
+    positions,
+    taps_held,
+    rings_held,
+    passed_in,
+    field_in,
+    exit_out,
+    probe,
+    taps,
+    rings,
+    field,
+    passed,
+    waves,
+    load_sem,
+    store_sem,
 ):
     probe_id = lax.axis_index("row") * lax.axis_size("beam") + lax.axis_index("beam")
-    loads = []
+    loads, others = [], []
     end = 0
     for n in range(FULL_BLOCKS + 1):
         start, end = end, min(n * BLOCK + BLOCK_IN, PASSED)
@@ -681,6 +790,10 @@
             )
         )
         loads[n].start()
+        if n == 0:
+            for m, pair in enumerate(((taps_held, taps), (rings_held, rings), (field_in, field))):
+                others.append(pltpu.make_async_copy(*pair, load_sem.at[FULL_BLOCKS + 1 + m]))
+                others[m].start()
     spare = passed.shape[2] - PASSED
     passed[:, :, PASSED:, :] = jnp.zeros((2, 2, spare, NPIX), BF16)
 
@@ -708,6 +821,7 @@
         )
         stores[-1].start()
 
+    others[0].wait()
     for block in range(FULL_BLOCKS):
         loads[block].wait()
         start = block * BLOCK
@@ -715,9 +829,12 @@
         for beam in range(2):
             mixed = dot(taps[...], block_of(beam, start))
             parts.append(split(mixed[:BLOCK], mixed[BLOCK:]))
+        if block == 0:
+            others[1].wait()
         write(propagate(parts, rings), start, BLOCK)
 
     loads[FULL_BLOCKS].wait()
+    others[2].wait()
     left = jnp.concatenate([taps[:WIN], taps[BLOCK : BLOCK + WIN]])
     parts = []
     for mixed in [dot(left, block_of(beam, TAIL)) for beam in range(2)] + [dot(left, field[...])]:
@@ -746,12 +863,15 @@
             jax.ShapeDtypeStruct((2, NPIX // 2, 2 * NPIX), BF16),
             jax.ShapeDtypeStruct((1, 1, WIN, 2 * WIN), F32),
         ),
-        in_specs=[smem, vmem, vmem, anywhere, vmem],
+        in_specs=[smem] + [anywhere] * 4,
         out_specs=(anywhere, vmem),
         scratch_shapes=[
+            pltpu.VMEM((2 * BLOCK, 2 * BLOCK_IN), BF16),
+            pltpu.VMEM((RINGS, 2 * QUARTER, 2 * QUARTER), BF16),
+            pltpu.VMEM((2 * BLOCK_IN, NPIX), BF16),
             pltpu.VMEM((2, 2, TAIL + BLOCK_IN, NPIX), BF16),
             pltpu.VMEM((2, NPIX // 2, 2 * NPIX), BF16),
-            pltpu.SemaphoreType.DMA((FULL_BLOCKS + 1,)),
+            pltpu.SemaphoreType.DMA((FULL_BLOCKS + 4,)),
             pltpu.SemaphoreType.DMA((FULL_BLOCKS + 1,)),
         ],
         compiler_params=pltpu.CompilerParams(vmem_limit_bytes=60 * 2**20),

time: 60.7 us -> 58.2 us (0.959)
  Pallas kernels: 59.9 us -> 57.4 us
    pallas_call x1, Pallas kernels: 50.3 us -> 48.9 us  [first_slice(): pl.pallas_call(first_kernel, out_shape=(jax.ShapeDtypeStruct((2, 2, PASSE...]
    pallas_call x1, Pallas kernels: 9.57 us -> 8.46 us  [second_slice(): pl.pallas_call(second_kernel, out_shape=(jax.ShapeDtypeStruct((2, NPIX //...]
where the time goes in v2:
time: 58.2 us; the launch traced here: 58 us
  Pallas kernels  57.4 us (99%)
  between operations  0.64 us (1%)
    pallas_call x1, Pallas kernels, first_slice(): pl.pallas_call(first_kernel, out_shape=(jax.ShapeDtypeStruct((2, 2, PASSE...  48.9 us
    pallas_call x1, Pallas kernels, second_slice(): pl.pallas_call(second_kernel, out_shape=(jax.ShapeDtypeStruct((2, NPIX //...  8.46 us

profile of v2, /device:TPU:1, one launch (start us, length us, event | category | flops | bytes accessed | tf_op | source)
XLA Modules:
  0.0 58.0 jit_solution(4544136492603959452)
XLA Ops:
  0.6 48.9 %first_slice.1 = (bf16[2,2,528,1024]{3,2,1,0:T(8,128)(2,1)}, bf16[256,1024]{1,0:T(8,128)(2,1)}) custom-call(s32[2]{0:T(128)} %owners.1, s32[2,2]{1,0:T(2,128)} %tilts.1, f32[2]{0:T(128)} %amplitude.1, f32[2]{0:T(128)} %angle.1, s32[2,128]{1,0:T(2,128)} %bitcast.1, s32[128]{0:T(128)} %offsets.1, bf16[1,512,1024]{2,1,0:T(8,128)(2,1)} %tiles.1, ...), custom_call_target="tpu_custom_call" | custom-call | tf_op jit(solution)/shard_map/first_slice/pallas_call | solution.py:703
  49.6 8.5 %second_slice.1 = (bf16[2,512,2048]{2,1,0:T(8,128)(2,1)}, f32[1,1,64,128]{3,2,1,0:T(8,128)}) custom-call(s32[2,128]{1,0:T(2,128)} %bitcast.2, bf16[224,256]{1,0:T(8,128)(2,1)} %constant.10.clone.taps_held, bf16[8,256,256]{2,1,0:T(8,128)(2,1)} %constant.11.clone.rings_held, bf16[2,2,528,1024]{3,2,1,0:T(8,128)(2,1)} %get-tuple-element.4.passed_in, ...), custom_call_target="tpu_custom_call" | custom-call | tf_op jit(solution)/shard_map/second_slice/pallas_call | solution.py:860

commit v3 on v2

--- a/solution.py
+++ b/solution.py
@@ -173,19 +173,27 @@
 
 
 def first_kernel(
+    owners_held,
+    tilts_held,
+    amplitude_held,
+    angle_held,
+    positions_held,
+    offsets_held,
+    tiles,
+    taps_real_held,
+    taps_imag_held,
+    taps_held,
+    rings_held,
+    passed_out,
+    field_out,
     owners,
     tilts,
     amplitude,
     angle,
     positions,
     offsets,
-    tiles,
     taps_real,
     taps_imag,
-    taps_held,
-    rings_held,
-    passed_out,
-    field_out,
     beams,
     own,
     other,
@@ -229,8 +237,6 @@
     piece = rows // 4
     probe_id = block * lax.axis_size("beam") + me
     row_start = block * rows
-    probe_row = positions[0, probe_id] - row_start
-    probe_column = positions[1, probe_id]
 
     def at(x, y, z, core):
         return ((z * 4 + y) * 4 + x) * 2 + core
@@ -250,6 +256,14 @@
     for partner in partners:
         pl.semaphore_signal(barrier, inc=1, device_id=partner, device_id_type=MESH)
 
+    held = (owners_held, tilts_held, amplitude_held, angle_held, positions_held, offsets_held)
+    here = (owners, tilts, amplitude, angle, positions, offsets, taps_real, taps_imag)
+    smalls = [
+        pltpu.make_async_copy(a, b, load_sem.at[STRIPS + 2 + n])
+        for n, (a, b) in enumerate(zip(held + (taps_real_held, taps_imag_held), here))
+    ]
+    for load in smalls:
+        load.start()
     loads = []
     for group, target in enumerate((sent, own)):
         for strip in range(half):
@@ -266,6 +280,11 @@
     loads.append(pltpu.make_async_copy(taps_held, taps, load_sem.at[STRIPS + 1]))
     for load in loads[:STRIPS]:
         load.start()
+
+    for load in smalls:
+        load.wait()
+    probe_row = positions[0, probe_id] - row_start
+    probe_column = positions[1, probe_id]
 
     lane = lax.broadcasted_iota(jnp.int32, (1, 1, LANES), 2)
     payload = jnp.zeros((1, 1, LANES), F32)
@@ -696,8 +715,6 @@
     half = STRIPS // 2
     rows = tiles.shape[1]
     piece = rows // 4
-    vmem = pl.BlockSpec(memory_space=pltpu.VMEM)
-    smem = pl.BlockSpec(memory_space=pltpu.SMEM)
     anywhere = pl.BlockSpec(memory_space=pl.ANY)
     reach = BLOCK_IN - 4 * RAD
     return pl.pallas_call(
@@ -706,9 +723,17 @@
             jax.ShapeDtypeStruct((2, 2, PASSED, NPIX), BF16),
             jax.ShapeDtypeStruct((2 * BLOCK_IN, NPIX), BF16),
         ),
-        in_specs=[smem] * 6 + [anywhere] + [vmem] * 2 + [anywhere] * 2,
+        in_specs=[anywhere] * 11,
         out_specs=(anywhere, anywhere),
         scratch_shapes=[
+            pltpu.SMEM(owners.shape, owners.dtype),
+            pltpu.SMEM(tilts.shape, tilts.dtype),
+            pltpu.SMEM(amplitude.shape, amplitude.dtype),
+            pltpu.SMEM(angle.shape, angle.dtype),
+            pltpu.SMEM(positions.shape, positions.dtype),
+            pltpu.SMEM(offsets.shape, offsets.dtype),
+            pltpu.VMEM(real.shape, F32),
+            pltpu.VMEM(real.shape, F32),
             pltpu.VMEM((lax.axis_size("beam"), 1, LANES), F32),
             pltpu.VMEM((half, rows, LANES), BF16),
             pltpu.VMEM((half, rows, LANES), BF16),
@@ -731,7 +756,7 @@
             pltpu.VMEM((2 * reach, NPIX), F32),
             pltpu.VMEM((2 * BLOCK_IN, NPIX), BF16),
             pltpu.VMEM((2, 2, PASSED, NPIX), BF16),
-            pltpu.SemaphoreType.DMA((STRIPS + 2,)),
+            pltpu.SemaphoreType.DMA((STRIPS + 10,)),
             pltpu.SemaphoreType.DMA((half,)),
             pltpu.SemaphoreType.DMA((half,)),
             pltpu.SemaphoreType.DMA((2, 13)),
@@ -764,13 +789,14 @@
 
 
 def second_kernel(
-    positions,
+    positions_held,
     taps_held,
     rings_held,
     passed_in,
     field_in,
     exit_out,
     probe,
+    positions,
     taps,
     rings,
     field,
@@ -780,6 +806,12 @@
     store_sem,
 ):
     probe_id = lax.axis_index("row") * lax.axis_size("beam") + lax.axis_index("beam")
+    pairs = (
+        (taps_held, taps),
+        (rings_held, rings),
+        (field_in, field),
+        (positions_held, positions),
+    )
     loads, others = [], []
     end = 0
     for n in range(FULL_BLOCKS + 1):
@@ -791,7 +823,7 @@
         )
         loads[n].start()
         if n == 0:
-            for m, pair in enumerate(((taps_held, taps), (rings_held, rings), (field_in, field))):
+            for m, pair in enumerate(pairs):
                 others.append(pltpu.make_async_copy(*pair, load_sem.at[FULL_BLOCKS + 1 + m]))
                 others[m].start()
     spare = passed.shape[2] - PASSED
@@ -835,6 +867,7 @@
 
     loads[FULL_BLOCKS].wait()
     others[2].wait()
+    others[3].wait()
     left = jnp.concatenate([taps[:WIN], taps[BLOCK : BLOCK + WIN]])
     parts = []
     for mixed in [dot(left, block_of(beam, TAIL)) for beam in range(2)] + [dot(left, field[...])]:
@@ -855,7 +888,6 @@
     real, imag = row_matrices()
     taps = np.block([[real, -imag], [imag, real]]).astype(ml_dtypes.bfloat16)
     vmem = pl.BlockSpec(memory_space=pltpu.VMEM)
-    smem = pl.BlockSpec(memory_space=pltpu.SMEM)
     anywhere = pl.BlockSpec(memory_space=pl.ANY)
     return pl.pallas_call(
         second_kernel,
@@ -863,15 +895,16 @@
             jax.ShapeDtypeStruct((2, NPIX // 2, 2 * NPIX), BF16),
             jax.ShapeDtypeStruct((1, 1, WIN, 2 * WIN), F32),
         ),
-        in_specs=[smem] + [anywhere] * 4,
+        in_specs=[anywhere] * 5,
         out_specs=(anywhere, vmem),
         scratch_shapes=[
+            pltpu.SMEM(positions.shape, positions.dtype),
             pltpu.VMEM((2 * BLOCK, 2 * BLOCK_IN), BF16),
             pltpu.VMEM((RINGS, 2 * QUARTER, 2 * QUARTER), BF16),
             pltpu.VMEM((2 * BLOCK_IN, NPIX), BF16),
             pltpu.VMEM((2, 2, TAIL + BLOCK_IN, NPIX), BF16),
             pltpu.VMEM((2, NPIX // 2, 2 * NPIX), BF16),
-            pltpu.SemaphoreType.DMA((FULL_BLOCKS + 4,)),
+            pltpu.SemaphoreType.DMA((FULL_BLOCKS + 5,)),
             pltpu.SemaphoreType.DMA((FULL_BLOCKS + 1,)),
         ],
         compiler_params=pltpu.CompilerParams(vmem_limit_bytes=60 * 2**20),

time: 58.2 us -> 56.7 us (0.974)
  Pallas kernels: 57.4 us -> 55.9 us
    pallas_call x1, Pallas kernels: 48.9 us -> 48.1 us  [first_slice(): pl.pallas_call(first_kernel, out_shape=(jax.ShapeDtypeStruct((2, 2, PASSE...]
    pallas_call x1, Pallas kernels: 8.46 us -> 7.78 us  [second_slice(): pl.pallas_call(second_kernel, out_shape=(jax.ShapeDtypeStruct((2, NPIX //...]
where the time goes in v3:
time: 56.7 us; the launch traced here: 56.6 us
  Pallas kernels  55.9 us (99%)
  between operations  0.64 us (1%)
    pallas_call x1, Pallas kernels, first_slice(): pl.pallas_call(first_kernel, out_shape=(jax.ShapeDtypeStruct((2, 2, PASSE...  48.1 us
    pallas_call x1, Pallas kernels, second_slice(): pl.pallas_call(second_kernel, out_shape=(jax.ShapeDtypeStruct((2, NPIX //...  7.78 us

profile of v3, /device:TPU:1, one launch (start us, length us, event | category | flops | bytes accessed | tf_op | source)
XLA Modules:
  0.0 56.6 jit_solution(1887777890164873111)
XLA Ops:
  0.6 48.1 %first_slice.1 = (bf16[2,2,528,1024]{3,2,1,0:T(8,128)(2,1)}, bf16[256,1024]{1,0:T(8,128)(2,1)}) custom-call(s32[2]{0:T(128)} %owners_held.1, s32[2,2]{1,0:T(2,128)} %tilts_held.1, f32[2]{0:T(128)} %amplitude_held.1, f32[2]{0:T(128)} %angle_held.1, s32[2,128]{1,0:T(2,128)} %bitcast.1, s32[128]{0:T(128)} %offsets_held.1, bf16[1,512,1024]{2,1,0:T(8,128)(2,1)} %tiles.1, ...), custom_call_target="tpu_custom_call" | custom-call | tf_op jit(solution)/shard_map/first_slice/pallas_call | solution.py:720
  48.8 7.8 %second_slice.1 = (bf16[2,512,2048]{2,1,0:T(8,128)(2,1)}, f32[1,1,64,128]{3,2,1,0:T(8,128)}) custom-call(s32[2,128]{1,0:T(2,128)} %bitcast.2, bf16[224,256]{1,0:T(8,128)(2,1)} %constant.10.clone.taps_held, bf16[8,256,256]{2,1,0:T(8,128)(2,1)} %constant.11.clone.rings_held, bf16[2,2,528,1024]{3,2,1,0:T(8,128)(2,1)} %get-tuple-element.4.passed_in, ...), custom_call_target="tpu_custom_call" | custom-call | tf_op jit(solution)/shard_map/second_slice/pallas_call | solution.py:892

commit v4 on v3

--- a/solution.py
+++ b/solution.py
@@ -585,42 +585,55 @@
         c, s = cos_sin(dot(chosen, held))
         return c.astype(BF16).astype(F32), s.astype(BF16).astype(F32)
 
+    def factors0(side):
+        def factors(step, carry):
+            held = pl.ds(pl.multiple_of(step * STEP, 16), STEP)
+            for n in range(half):
+                at_strip = side * half + n
+                columns = pl.ds(pl.multiple_of(at_strip * LANES, LANES), LANES)
+                c, s = cos_sin(kept[0, at_strip, held, :].astype(F32))
+                factor0[0, held, columns] = c.astype(BF16)
+                factor0[1, held, columns] = s.astype(BF16)
+            return carry
+
+        lax.fori_loop(0, factor0.shape[1] // STEP, factors, 0)
+
+    def probe_in(side):
+        for n in range(half // 2):
+            pair = side * (half // 2) + n
+            columns = pl.ds(pl.multiple_of(pair * 2 * LANES, 2 * LANES), 2 * LANES)
+            fr, fi = window(0, probe_row, reach, pair)
+            r, i = incident[:reach, columns], incident[reach:, columns]
+            field[:reach, columns] = (r * fr - i * fi).astype(BF16)
+            field[BLOCK_IN : BLOCK_IN + reach, columns] = (r * fi + i * fr).astype(BF16)
+
+    field[...] = jnp.zeros(field.shape, BF16)
+    factors0(core)
+    probe_in(core)
     for copy in twin_copies[0]:
         copy.wait_recv()
-
-    def factors0(step, carry):
-        held = pl.ds(pl.multiple_of(step * STEP, 16), STEP)
-        for strip in range(STRIPS):
-            columns = slice(strip * LANES, (strip + 1) * LANES)
-            c, s = cos_sin(kept[0, strip, held, :].astype(F32))
-            factor0[0, held, columns] = c.astype(BF16)
-            factor0[1, held, columns] = s.astype(BF16)
-        return carry
-
-    lax.fori_loop(0, factor0.shape[1] // STEP, factors0, 0)
+    factors0(1 - core)
     back_to_twin(1)
-    field[...] = jnp.zeros(field.shape, BF16)
-    for pair in range(STRIPS // 2):
-        columns = slice(pair * 2 * LANES, (pair + 1) * 2 * LANES)
-        fr, fi = window(0, probe_row, reach, pair)
-        r, i = incident[:reach, columns], incident[reach:, columns]
-        field[:reach, columns] = (r * fr - i * fi).astype(BF16)
-        field[BLOCK_IN : BLOCK_IN + reach, columns] = (r * fi + i * fr).astype(BF16)
-
+
+    def factors1(side):
+        def factors(step, carry):
+            start = pl.multiple_of(step * STEP, 16)
+            for n in range(half):
+                at_strip = side * half + n
+                columns = pl.ds(pl.multiple_of(at_strip * LANES, LANES), LANES)
+                values = kept[1, at_strip, pl.ds(start, STEP + 16), :].astype(F32)
+                c, s = cos_sin(values[RAD : RAD + STEP])
+                factor1[0, pl.ds(start, STEP), columns] = c.astype(BF16)
+                factor1[1, pl.ds(start, STEP), columns] = s.astype(BF16)
+            return carry
+
+        lax.fori_loop(0, factor1.shape[1] // STEP, factors, 0)
+
+    factors1(core)
+    probe_in(1 - core)
     for copy in twin_copies[1]:
         copy.wait_recv()
-
-    def factors1(step, carry):
-        start = pl.multiple_of(step * STEP, 16)
-        for strip in range(STRIPS):
-            columns = slice(strip * LANES, (strip + 1) * LANES)
-            values = kept[1, strip, pl.ds(start, STEP + 16), :].astype(F32)[RAD : RAD + STEP]
-            c, s = cos_sin(values)
-            factor1[0, pl.ds(start, STEP), columns] = c.astype(BF16)
-            factor1[1, pl.ds(start, STEP), columns] = s.astype(BF16)
-        return carry
-
-    lax.fori_loop(0, factor1.shape[1] // STEP, factors1, 0)
+    factors1(1 - core)
     for load in loads[STRIPS:]:
         load.wait()
 

time: 56.7 us -> 56.4 us (level)
  no operation moved by 1% of the time
where the time goes in v4:
time: 56.4 us; the launch traced here: 56.3 us
  Pallas kernels  55.6 us (99%)
  between operations  0.64 us (1%)
    pallas_call x1, Pallas kernels, first_slice(): pl.pallas_call(first_kernel, out_shape=(jax.ShapeDtypeStruct((2, 2, PASSE...  47.9 us
    pallas_call x1, Pallas kernels, second_slice(): pl.pallas_call(second_kernel, out_shape=(jax.ShapeDtypeStruct((2, NPIX //...  7.79 us

profile of v4, /device:TPU:1, one launch (start us, length us, event | category | flops | bytes accessed | tf_op | source)
XLA Modules:
  0.0 56.3 jit_solution(10125343071132756773)
XLA Ops:
  0.6 47.9 %first_slice.1 = (bf16[2,2,528,1024]{3,2,1,0:T(8,128)(2,1)}, bf16[256,1024]{1,0:T(8,128)(2,1)}) custom-call(s32[2]{0:T(128)} %owners_held.1, s32[2,2]{1,0:T(2,128)} %tilts_held.1, f32[2]{0:T(128)} %amplitude_held.1, f32[2]{0:T(128)} %angle_held.1, s32[2,128]{1,0:T(2,128)} %bitcast.1, s32[128]{0:T(128)} %offsets_held.1, bf16[1,512,1024]{2,1,0:T(8,128)(2,1)} %tiles.1, ...), custom_call_target="tpu_custom_call" | custom-call | tf_op jit(solution)/shard_map/first_slice/pallas_call | solution.py:733
  48.5 7.8 %second_slice.1 = (bf16[2,512,2048]{2,1,0:T(8,128)(2,1)}, f32[1,1,64,128]{3,2,1,0:T(8,128)}) custom-call(s32[2,128]{1,0:T(2,128)} %bitcast.2, bf16[224,256]{1,0:T(8,128)(2,1)} %constant.10.clone.taps_held, bf16[8,256,256]{2,1,0:T(8,128)(2,1)} %constant.11.clone.rings_held, bf16[2,2,528,1024]{3,2,1,0:T(8,128)(2,1)} %get-tuple-element.4.passed_in, ...), custom_call_target="tpu_custom_call" | custom-call | tf_op jit(solution)/shard_map/second_slice/pallas_call | solution.py:905

commit v5 on v4

--- a/solution.py
+++ b/solution.py
@@ -197,7 +197,6 @@
     beams,
     own,
     other,
-    sent,
     masked,
     arrived1,
     summed1,
@@ -264,21 +263,17 @@
     ]
     for load in smalls:
         load.start()
-    loads = []
-    for group, target in enumerate((sent, own)):
-        for strip in range(half):
-            side = 1 - core if group == 0 else core
-            column = pl.multiple_of((side * half + strip) * LANES, LANES)
-            loads.append(
-                pltpu.make_async_copy(
-                    tiles.at[0, :, pl.ds(column, LANES)],
-                    target.at[strip],
-                    load_sem.at[group * half + strip],
-                )
-            )
+    def strip_held(side, strip):
+        column = pl.multiple_of((side * half + strip) * LANES, LANES)
+        return tiles.at[0, :, pl.ds(column, LANES)]
+
+    loads = [
+        pltpu.make_async_copy(strip_held(core, strip), own.at[strip], load_sem.at[strip])
+        for strip in range(half)
+    ]
     loads.append(pltpu.make_async_copy(rings_held, rings, load_sem.at[STRIPS]))
     loads.append(pltpu.make_async_copy(taps_held, taps, load_sem.at[STRIPS + 1]))
-    for load in loads[:STRIPS]:
+    for load in loads[:half]:
         load.start()
 
     for load in smalls:
@@ -340,21 +335,19 @@
 
     chunk = beam_chunk(1)
     beam_copies = [send(chunk, chunk, beam_send.at[0], beam_recv.at[0], (twin, block))]
-    swaps = []
-    for strip in range(half):
-        loads[strip].wait()
-        swaps.append(
-            send(
-                sent.at[strip],
-                other.at[strip],
-                swap_send.at[strip],
-                swap_recv.at[strip],
-                (twin, block),
-            )
-        )
-    for load in loads[half:STRIPS]:
+    swaps = [
+        send(
+            strip_held(1 - core, strip),
+            other.at[strip],
+            swap_send.at[strip],
+            swap_recv.at[strip],
+            (twin, block),
+        )
+        for strip in range(half)
+    ]
+    for load in loads[:half]:
         load.wait()
-    for load in loads[STRIPS:]:
+    for load in loads[half:]:
         load.start()
 
     def beam_step(size, devices, slot):
@@ -634,7 +627,7 @@
     for copy in twin_copies[1]:
         copy.wait_recv()
     factors1(1 - core)
-    for load in loads[STRIPS:]:
+    for load in loads[half:]:
         load.wait()
 
     def turned(mixed, count, beam, block):
@@ -748,7 +741,6 @@
             pltpu.VMEM(real.shape, F32),
             pltpu.VMEM(real.shape, F32),
             pltpu.VMEM((lax.axis_size("beam"), 1, LANES), F32),
-            pltpu.VMEM((half, rows, LANES), BF16),
             pltpu.VMEM((half, rows, LANES), BF16),
             pltpu.VMEM((half, rows, LANES), BF16),
             pltpu.VMEM((2, half, rows, LANES), BF16),

time: 56.4 us -> 56.6 us (level)
  no operation moved by 1% of the time
where the time goes in v5:
time: 56.6 us; the launch traced here: 56.5 us
  Pallas kernels  55.8 us (99%)
  between operations  0.64 us (1%)
    pallas_call x1, Pallas kernels, first_slice(): pl.pallas_call(first_kernel, out_shape=(jax.ShapeDtypeStruct((2, 2, PASSE...  48.1 us
    pallas_call x1, Pallas kernels, second_slice(): pl.pallas_call(second_kernel, out_shape=(jax.ShapeDtypeStruct((2, NPIX //...  7.78 us

profile of v5, /device:TPU:1, one launch (start us, length us, event | category | flops | bytes accessed | tf_op | source)
XLA Modules:
  0.0 56.5 jit_solution(679432924418305393)
XLA Ops:
  0.6 48.1 %first_slice.1 = (bf16[2,2,528,1024]{3,2,1,0:T(8,128)(2,1)}, bf16[256,1024]{1,0:T(8,128)(2,1)}) custom-call(s32[2]{0:T(128)} %owners_held.1, s32[2,2]{1,0:T(2,128)} %tilts_held.1, f32[2]{0:T(128)} %amplitude_held.1, f32[2]{0:T(128)} %angle_held.1, s32[2,128]{1,0:T(2,128)} %bitcast.1, s32[128]{0:T(128)} %offsets_held.1, bf16[1,512,1024]{2,1,0:T(8,128)(2,1)} %tiles.1, ...), custom_call_target="tpu_custom_call" | custom-call | tf_op jit(solution)/shard_map/first_slice/pallas_call | solution.py:726
  48.7 7.8 %second_slice.1 = (bf16[2,512,2048]{2,1,0:T(8,128)(2,1)}, f32[1,1,64,128]{3,2,1,0:T(8,128)}) custom-call(s32[2,128]{1,0:T(2,128)} %bitcast.2, bf16[224,256]{1,0:T(8,128)(2,1)} %constant.10.clone.taps_held, bf16[8,256,256]{2,1,0:T(8,128)(2,1)} %constant.11.clone.rings_held, bf16[2,2,528,1024]{3,2,1,0:T(8,128)(2,1)} %get-tuple-element.4.passed_in, ...), custom_call_target="tpu_custom_call" | custom-call | tf_op jit(solution)/shard_map/second_slice/pallas_call | solution.py:897
